TPU v7x, 128 devices: a whole 4x4x4 slice. The times are simulated.
128 devices in a mesh: rep: 8 (over x_lo, z), shard: 16 (over y, x_hi, core).
Axes of the slice: x: 4 (x_hi: 2, x_lo: 2; x = x_hi * 2 + x_lo), y: 4, z: 4, core: 2. Of those that a mesh axis runs over, the one named last changes fastest.
Arguments:
- hidden_in: bfloat16 [32768, 2048], P(('rep', 'shard')), may hold values from -6 to 6
- cotangent: bfloat16 [32768, 2048], P(('rep', 'shard')), may hold values from -6 to 6
- segment_ids: int32 [32768], P('rep'), may hold values from 0 to 2, as said below
- positions: int32 [32768], P('rep'), may hold values from 0 to 3583, as said below
- attn_gain: float32 [2048], P('shard'), may hold values from 0.25 to 1.75
- query_gain: float32 [128], replicated, may hold values from 0.25 to 1.75
- key_gain: float32 [128], replicated, may hold values from 0.25 to 1.75
- query_weight: float32 [2048, 2048], P('shard'), may hold values from -0.125 to 0.125
- key_weight: float32 [2048, 1024], P('shard'), may hold values from -0.125 to 0.125
- value_weight: float32 [2048, 1024], P('shard'), may hold values from -0.125 to 0.125
- out_weight: float32 [2048, 2048], P('shard'), may hold values from -3 to 3
- mlp_gain: float32 [2048], P('shard'), may hold values from 0.25 to 1.75
- gate_weight: float32 [2048, 6144], P('shard'), may hold values from -0.125 to 0.125
- up_weight: float32 [2048, 6144], P('shard'), may hold values from -0.125 to 0.125
- down_weight: float32 [2048, 6144], P('shard'), may hold values from -0.078125 to 0.078125
Outputs:
- output: bfloat16 [32768, 2048], P(('rep', 'shard'))
- hidden_grad: bfloat16 [32768, 2048], P(('rep', 'shard'))
- attn_gain_grad: float32 [2048], P('shard')
- query_gain_grad: float32 [128], replicated
- key_gain_grad: float32 [128], replicated
- query_weight_grad: float32 [2048, 2048], P('shard')
- key_weight_grad: float32 [2048, 1024], P('shard')
- value_weight_grad: float32 [2048, 1024], P('shard')
- out_weight_grad: float32 [2048, 2048], P('shard')
- mlp_gain_grad: float32 [2048], P('shard')
- gate_weight_grad: float32 [2048, 6144], P('shard')
- up_weight_grad: float32 [2048, 6144], P('shard')
- down_weight_grad: float32 [2048, 6144], P('shard')
Inputs may be any that keep to these rules, and one draw needn't show every extreme that they name: `segment_ids`: within the 4096 rows of each index of rep, one prompt of 3072 rows (segment 0) and 2 continuations of 512 rows (segments 1 to 2) are laid out; each index of shard holds 256 consecutive rows of the order prompt, continuation 1, ..., and these runs are placed on the devices in a drawn order. Prompt rows have positions 0 to 3071 in order; continuation rows have positions 3072 to 3583 in order, in the layout of segment_ids.
All inputs are finite; a program needn't handle non-finite values.
Results may differ from a plain program's by a relative error of at most 0.025.
Values may be sent and summed in bfloat16 or wider, within the bound.
No kernel may reach another device: no remote copies, remote signals or barrier semaphores. Data moves between devices by JAX's collectives and lax.ppermute only.
A program may use at most 384 MiB of HBM per device.

v0:
```python
import jax
import jax.numpy as jnp
from jax import lax
from jax.sharding import PartitionSpec as P

HEADS = 16
KV_HEADS = 8
HEAD_DIM = 128
Q_DIM = 2048
KV_DIM = 1024
norm_eps = 1e-06
rope_base = 1000000.0
masked_score = -1e30
contract_first = (((0,), (0,)), ((), ()))
contract_last = (((1,), (1,)), ((), ()))


def normalize(values):
    return values * lax.rsqrt(jnp.mean(values * values, axis=-1, keepdims=True) + norm_eps)


def scaled_norm(values, scale):
    return normalize(values) * scale


def rotate(values, places):
    half_dim = values.shape[-1] // 2
    frequency = rope_base ** (-2.0 * jnp.arange(half_dim, dtype=jnp.float32) / values.shape[-1])
    angles = places.astype(jnp.float32)[:, None] * frequency[None, :]
    cosine = jnp.cos(angles)[:, None, :]
    sine_part = jnp.sin(angles)[:, None, :]
    first_half = values[..., :half_dim]
    second_half = values[..., half_dim:]
    return jnp.concatenate(
        [
            first_half * cosine - second_half * sine_part,
            second_half * cosine + first_half * sine_part,
        ],
        axis=-1,
    )


def swiglu(gate_in, upper_in):
    return jax.nn.silu(gate_in) * upper_in


def owner_share(left, right):
    term = lax.dot_general(left, right, contract_first, preferred_element_type=jnp.float32)
    return lax.psum_scatter(
        term.astype(jnp.bfloat16), "shard", scatter_dimension=0, tiled=True
    ).astype(jnp.float32)


def local(
    hidden_in,
    cotangent,
    segment_ids,
    positions,
    attn_gain,
    query_gain,
    key_gain,
    query_weight,
    key_weight,
    value_weight,
    out_weight,
    mlp_gain,
    gate_weight,
    up_weight,
    down_weight,
):
    row_count = hidden_in.shape[0]
    own_rows = attn_gain.shape[0]
    my_index = lax.axis_index("shard")
    group_rows = segment_ids.shape[0]
    group_size = HEADS // KV_HEADS
    score_scale = HEAD_DIM ** (-0.5)
    own_segments = lax.dynamic_slice_in_dim(segment_ids, my_index * row_count, row_count)
    own_places = lax.dynamic_slice_in_dim(positions, my_index * row_count, row_count)
    hidden = hidden_in.astype(jnp.float32)
    gain_low, query_low, key_low, value_low, out_low = (
        lax.all_gather(attn_gain.astype(jnp.bfloat16), "shard", axis=0, tiled=True),
        lax.all_gather(query_weight.astype(jnp.bfloat16), "shard", axis=0, tiled=True),
        lax.all_gather(key_weight.astype(jnp.bfloat16), "shard", axis=0, tiled=True),
        lax.all_gather(value_weight.astype(jnp.bfloat16), "shard", axis=0, tiled=True),
        lax.all_gather(out_weight.astype(jnp.bfloat16), "shard", axis=0, tiled=True),
    )
    attn_scale = gain_low.astype(jnp.float32)
    first_in = scaled_norm(hidden, attn_scale).astype(jnp.bfloat16)
    query_pre = jnp.dot(first_in, query_low, preferred_element_type=jnp.float32)
    key_pre = jnp.dot(first_in, key_low, preferred_element_type=jnp.float32)
    value_pre = jnp.dot(first_in, value_low, preferred_element_type=jnp.float32)

    def head_prep(query_part, key_part, query_scale, key_scale):
        query_out = rotate(
            normalize(query_part.reshape(row_count, HEADS, HEAD_DIM)) * query_scale, own_places
        )
        key_out = rotate(
            normalize(key_part.reshape(row_count, KV_HEADS, HEAD_DIM)) * key_scale, own_places
        )
        return (query_out, key_out)

    (queries, key_act), prep_back = jax.vjp(head_prep, query_pre, key_pre, query_gain, key_gain)
    key_send = key_act.astype(jnp.bfloat16).reshape(row_count, KV_DIM)
    value_send = value_pre.astype(jnp.bfloat16)
    key_all, value_all = (
        lax.all_gather(key_send, "shard", axis=0, tiled=True),
        lax.all_gather(value_send, "shard", axis=0, tiled=True),
    )
    visible = (positions[None, :] <= own_places[:, None]) & (
        (segment_ids[None, :] == 0) | (segment_ids[None, :] == own_segments[:, None])
    )
    tiled_mask = jnp.tile(visible, (group_size, 1))
    query_heads = (
        queries.astype(jnp.bfloat16)
        .reshape(row_count, KV_HEADS, group_size, HEAD_DIM)
        .transpose(1, 2, 0, 3)
        .reshape(KV_HEADS, group_size * row_count, HEAD_DIM)
    )

    def head_scores(head_index):
        head_keys = lax.dynamic_slice_in_dim(key_all, head_index * HEAD_DIM, HEAD_DIM, 1)
        raw_scores = (
            lax.dot_general(
                query_heads[head_index],
                head_keys,
                contract_last,
                preferred_element_type=jnp.float32,
            )
            * score_scale
        )
        return (jnp.where(tiled_mask, raw_scores, masked_score), head_keys)

    def forward_head(head_index):
        scores, head_keys = head_scores(head_index)
        row_max = jnp.max(scores, axis=-1, keepdims=True)
        unscaled = jnp.exp(scores - row_max)
        row_total = jnp.sum(unscaled, axis=-1, keepdims=True)
        probabilities = unscaled / row_total
        head_values = lax.dynamic_slice_in_dim(value_all, head_index * HEAD_DIM, HEAD_DIM, 1)
        head_mixed = jnp.dot(
            probabilities.astype(jnp.bfloat16), head_values, preferred_element_type=jnp.float32
        )
        return (head_mixed, row_max + jnp.log(row_total))

    mixed_heads, log_totals = lax.map(forward_head, jnp.arange(KV_HEADS))
    mixed_out = (
        mixed_heads.reshape(KV_HEADS, group_size, row_count, HEAD_DIM)
        .transpose(2, 0, 1, 3)
        .reshape(row_count, Q_DIM)
    )
    mixed_low = mixed_out.astype(jnp.bfloat16)
    attn_out = lax.dot_general(
        mixed_low, out_low, contract_last, preferred_element_type=jnp.float32
    )
    middle = hidden + attn_out
    second_norm = normalize(middle)
    gate_cast = gate_weight.astype(jnp.bfloat16)
    up_cast = up_weight.astype(jnp.bfloat16)
    down_cast = down_weight.astype(jnp.bfloat16)
    gain_piece = lax.all_gather(mlp_gain.astype(jnp.bfloat16), "shard", axis=0, tiled=True)
    gate_piece = lax.all_gather(gate_cast, "shard", axis=0, tiled=True)
    up_piece = lax.all_gather(up_cast, "shard", axis=0, tiled=True)
    columns = second_norm
    piece_in = (columns * gain_piece.astype(jnp.float32)).astype(jnp.bfloat16)
    gate_act = jnp.dot(piece_in, gate_piece, preferred_element_type=jnp.float32)
    up_act = jnp.dot(piece_in, up_piece, preferred_element_type=jnp.float32)
    mlp_scale = gain_piece.astype(jnp.float32)
    activated, swiglu_back = jax.vjp(swiglu, gate_act, up_act)
    inner_low = activated.astype(jnp.bfloat16)
    mlp_out = lax.dot_general(
        inner_low,
        lax.all_gather(down_cast, "shard", axis=0, tiled=True),
        contract_last,
        preferred_element_type=jnp.float32,
    )
    output = (middle + mlp_out).astype(jnp.bfloat16)
    cot_float = cotangent.astype(jnp.float32)
    columns = cotangent
    inner_grad = jnp.dot(
        columns,
        lax.all_gather(down_cast, "shard", axis=0, tiled=True),
        preferred_element_type=jnp.float32,
    )
    gate_grad, upper_grad = swiglu_back(inner_grad)
    gate_grad_low = gate_grad.astype(jnp.bfloat16)
    upper_grad_low = upper_grad.astype(jnp.bfloat16)
    block = lax.dot_general(
        gate_grad_low,
        lax.all_gather(gate_cast, "shard", axis=0, tiled=True),
        contract_last,
        preferred_element_type=jnp.float32,
    ) + lax.dot_general(
        upper_grad_low,
        lax.all_gather(up_cast, "shard", axis=0, tiled=True),
        contract_last,
        preferred_element_type=jnp.float32,
    )
    _, second_back = jax.vjp(scaled_norm, middle, mlp_scale)
    middle_part, mlp_gain_part = second_back(block)
    middle_grad = cot_float + middle_part
    middle_low = middle_grad.astype(jnp.bfloat16)
    mixed_grad_low = jnp.dot(middle_low, out_low, preferred_element_type=jnp.float32).astype(
        jnp.bfloat16
    )
    mixed_grad_heads = (
        mixed_grad_low.reshape(row_count, KV_HEADS, group_size, HEAD_DIM)
        .transpose(1, 2, 0, 3)
        .reshape(KV_HEADS, group_size * row_count, HEAD_DIM)
    )

    def backward_head(head_index, running):
        query_grads, key_grads, value_grads = running
        scores, head_keys = head_scores(head_index)
        probabilities = jnp.exp(scores - log_totals[head_index])
        head_values = lax.dynamic_slice_in_dim(value_all, head_index * HEAD_DIM, HEAD_DIM, 1)
        head_out_grad = mixed_grad_heads[head_index]
        prob_grad = lax.dot_general(
            head_out_grad, head_values, contract_last, preferred_element_type=jnp.float32
        )
        score_grad = probabilities * (
            prob_grad - jnp.sum(probabilities * prob_grad, axis=-1, keepdims=True)
        )
        score_low = score_grad.astype(jnp.bfloat16)
        query_part = jnp.dot(score_low, head_keys, preferred_element_type=jnp.float32) * score_scale
        key_part = (
            lax.dot_general(
                score_low,
                query_heads[head_index],
                contract_first,
                preferred_element_type=jnp.float32,
            )
            * score_scale
        )
        value_part = lax.dot_general(
            probabilities.astype(jnp.bfloat16),
            head_out_grad,
            contract_first,
            preferred_element_type=jnp.float32,
        )
        return (
            lax.dynamic_update_index_in_dim(query_grads, query_part, head_index, 0),
            lax.dynamic_update_slice_in_dim(key_grads, key_part, head_index * HEAD_DIM, 1),
            lax.dynamic_update_slice_in_dim(value_grads, value_part, head_index * HEAD_DIM, 1),
        )

    start_grads = (
        jnp.zeros((KV_HEADS, group_size * row_count, HEAD_DIM), jnp.float32),
        jnp.zeros((group_rows, KV_DIM), jnp.float32),
        jnp.zeros((group_rows, KV_DIM), jnp.float32),
    )
    query_grads, key_grads, value_grads = lax.fori_loop(0, KV_HEADS, backward_head, start_grads)
    key_grad_own, value_grad_own = (
        lax.psum_scatter(
            key_grads.astype(jnp.bfloat16), "shard", scatter_dimension=0, tiled=True
        ).astype(jnp.float32),
        lax.psum_scatter(
            value_grads.astype(jnp.bfloat16), "shard", scatter_dimension=0, tiled=True
        ).astype(jnp.float32),
    )
    query_grad = (
        query_grads.reshape(KV_HEADS, group_size, row_count, HEAD_DIM)
        .transpose(2, 0, 1, 3)
        .reshape(row_count, HEADS, HEAD_DIM)
    )
    query_pre_grad, key_pre_grad, query_gain_part, key_gain_part = prep_back(
        (query_grad, key_grad_own.reshape(row_count, KV_HEADS, HEAD_DIM))
    )
    query_pre_low = query_pre_grad.astype(jnp.bfloat16)
    key_pre_low = key_pre_grad.astype(jnp.bfloat16)
    value_pre_low = value_grad_own.astype(jnp.bfloat16)
    first_grad = (
        lax.dot_general(query_pre_low, query_low, contract_last, preferred_element_type=jnp.float32)
        + lax.dot_general(key_pre_low, key_low, contract_last, preferred_element_type=jnp.float32)
        + lax.dot_general(
            value_pre_low, value_low, contract_last, preferred_element_type=jnp.float32
        )
    )
    _, first_back = jax.vjp(scaled_norm, hidden, attn_scale)
    hidden_part, attn_gain_part = first_back(first_grad)
    hidden_grad = (middle_grad + hidden_part).astype(jnp.bfloat16)
    query_share = owner_share(first_in, query_pre_low)
    key_share = owner_share(first_in, key_pre_low)
    value_share = owner_share(first_in, value_pre_low)
    out_share = owner_share(middle_low, mixed_low)
    gate_share, up_share, down_share = (
        owner_share(piece_in, gate_grad_low),
        owner_share(piece_in, upper_grad_low),
        owner_share(cotangent, inner_low),
    )
    gain_totals = lax.psum(
        (attn_gain_part, mlp_gain_part, query_gain_part, key_gain_part), ("rep", "shard")
    )
    attn_gain_out = lax.dynamic_slice_in_dim(gain_totals[0], my_index * own_rows, own_rows)
    mlp_gain_out = lax.dynamic_slice_in_dim(gain_totals[1], my_index * own_rows, own_rows)
    totals = (
        lax.psum(query_share.astype(jnp.bfloat16), "rep").astype(jnp.float32),
        lax.psum(key_share.astype(jnp.bfloat16), "rep").astype(jnp.float32),
        lax.psum(value_share.astype(jnp.bfloat16), "rep").astype(jnp.float32),
        lax.psum(out_share.astype(jnp.bfloat16), "rep").astype(jnp.float32),
        lax.psum(gate_share.astype(jnp.bfloat16), "rep").astype(jnp.float32),
        lax.psum(up_share.astype(jnp.bfloat16), "rep").astype(jnp.float32),
        lax.psum(down_share.astype(jnp.bfloat16), "rep").astype(jnp.float32),
    )
    return (
        output,
        hidden_grad,
        attn_gain_out,
        gain_totals[2],
        gain_totals[3],
        totals[0],
        totals[1],
        totals[2],
        totals[3],
        mlp_gain_out,
        totals[4],
        totals[5],
        totals[6],
    )


def solution(mesh):
    in_specs = (
        P(("rep", "shard"), None),
        P(("rep", "shard"), None),
        P("rep"),
        P("rep"),
        P("shard"),
        P(),
        P(),
        P("shard", None),
        P("shard", None),
        P("shard", None),
        P("shard", None),
        P("shard"),
        P("shard", None),
        P("shard", None),
        P("shard", None),
    )
    out_specs = (
        P(("rep", "shard"), None),
        P(("rep", "shard"), None),
        P("shard"),
        P(),
        P(),
        P("shard", None),
        P("shard", None),
        P("shard", None),
        P("shard", None),
        P("shard"),
        P("shard", None),
        P("shard", None),
        P("shard", None),
    )
    return jax.shard_map(local, mesh=mesh, in_specs=in_specs, out_specs=out_specs, check_vma=False)
```

profile of v0, /device:TPU:1, one launch (start us, length us, event | category | flops | bytes accessed | tf_op | source)
XLA Modules:
  0.0 2547.6 jit_solution(4251775933046974446)
XLA Ops:
  13.2 25.6 %all-gather = bf16[16,1,128]{2,1,0:T(2,128)(2,1)S(1)} all-gather(bf16[1,1,128]{2,1,0:T(2,128)(2,1)S(1)} %convert_bitcast_fusion.3), channel_id=1, replica_groups=mesh['rep'=8,'shard'=16] {'shard'}, dimensions={0}, use_global_device_ids=true | all-gather | bytes 4352 | tf_op jit(solution)/shard_map/all_gather | solution.py:81
  40.4 29.4 %all-gather.14.cloned.1.call-done = bf16[2048,1024]{1,0:T(8,128)(2,1)} async-done(((bf16[128,1024]{1,0:T(8,128)(2,1)}), bf16[2048,1024]{1,0:T(8,128)(2,1)}) %all-gather.14.cloned.1.call-update) | async-done | bytes 4194320 | tf_op jit(solution)/shard_map/all_gather | solution.py:83
  76.2 49.7 %all-gather.18.cloned.1.call-done = bf16[2048,1024]{1,0:T(8,128)(2,1)} async-done(((bf16[128,1024]{1,0:T(8,128)(2,1)}), bf16[2048,1024]{1,0:T(8,128)(2,1)}) %all-gather.18.cloned.1.call-update) | async-done | bytes 4194320 | tf_op jit(solution)/shard_map/all_gather | solution.py:84
  141.4 19.9 all-gather.1
  163.5 36.2 %all-gather.12.cloned.1.call-done = bf16[2048,2048]{1,0:T(8,128)(2,1)} async-done(((bf16[128,2048]{1,0:T(8,128)(2,1)}), bf16[2048,2048]{1,0:T(8,128)(2,1)}) %all-gather.12.cloned.1.call-update) | async-done | bytes 8388624 | tf_op jit(solution)/shard_map/all_gather | solution.py:82
  214.9 58.4 %all-gather.16.cloned.1.call-done = bf16[4096,1024]{1,0:T(8,128)(2,1)} async-done(((bf16[256,1024]{1,0:T(8,128)(2,1)}), bf16[4096,1024]{1,0:T(8,128)(2,1)}) %all-gather.16.cloned.1.call-update) | async-done | bytes 8388624 | tf_op jit(solution)/shard_map/all_gather | solution.py:106
  273.4 73.6 %all-gather.20.cloned.1.call-done = bf16[4096,1024]{1,0:T(8,128)(2,1)} async-done(((bf16[256,1024]{1,0:T(8,128)(2,1)}), bf16[4096,1024]{1,0:T(8,128)(2,1)}) %all-gather.20.cloned.1.call-update) | async-done | bytes 8388624 | tf_op jit(solution)/shard_map/all_gather | solution.py:107
  347.0 118.2 %while.33 = (s32[]{:T(128)}, bf16[8,512,128]{2,1,0:T(8,128)(2,1)}, f32[8,512,1]{1,2,0:T(1,128)S(1)}, s32[8]{0:T(128)S(1)}, bf16[8,512,128]{2,1,0:T(8,128)(2,1)},...) while((s32[]{:T(128)}, bf16[8,512,128]{2,1,0:T(8,128)(2,1)}, ...), condition=%wide.region_6.7_spmd.clone.clone, body=%wide.region_3.6_spmd.clone.sunk.clone | while | flops 1098907136 | bytes 39211712 | solution.py:145
  475.4 93.1 %all-gather.24.cloned.1.call-done = bf16[2048,6144]{1,0:T(8,128)(2,1)} async-done(((bf16[128,6144]{1,0:T(8,128)(2,1)}), bf16[2048,6144]{1,0:T(8,128)(2,1)}) %all-gather.24.cloned.1.call-update) | async-done | bytes 25165840 | tf_op jit(solution)/shard_map/all_gather | solution.py:161
  583.2 133.5 %all-gather.26.cloned.1.call-done = bf16[2048,6144]{1,0:T(8,128)(2,1)} async-done(((bf16[128,6144]{1,0:T(8,128)(2,1)}), bf16[2048,6144]{1,0:T(8,128)(2,1)}) %all-gather.26.cloned.1.call-update) | async-done | bytes 25165840 | tf_op jit(solution)/shard_map/all_gather | solution.py:162
  731.1 133.9 %all-gather.28.cloned.1.call-done = bf16[2048,6144]{1,0:T(8,128)(2,1)} async-done(((bf16[128,6144]{1,0:T(8,128)(2,1)}), bf16[2048,6144]{1,0:T(8,128)(2,1)}) %all-gather.28.cloned.1.call-update) | async-done | bytes 25165840 | tf_op jit(solution)/shard_map/all_gather | solution.py:172
  865.0 18.8 multiply_convert_fusion.1
  934.6 252.0 %while.34 = (s32[]{:T(128)}, f32[8,512,128]{2,1,0:T(8,128)}, bf16[4096,1024]{1,0:T(8,128)(2,1)}, bf16[4096,1024]{1,0:T(8,128)(2,1)}, bf16[8,512,128]{2,1,0:T(8,1...) while((s32[]{:T(128)}, f32[8,512,128]{2,1,0:T(8,128)}, ...), condition=%wide.region_11.12_spmd.clone.clone, body=%wide.region_9.11_spmd.clone.sunk.clone | while | flops 2703818240 | bytes 105657016 | solution.py:251
  1204.5 32.8 %copy.74 = bf16[2048,6144]{1,0:T(8,128)(2,1)} copy(bf16[2048,6144]{0,1:T(8,128)(2,1)} %convert_bitcast_fusion) | data formatting | bytes 50331648
  1295.7 95.0 %reduce-scatter.14.cloned.1.call-done = bf16[256,1024]{1,0:T(8,128)(2,1)} async-done(((bf16[4096,1024]{1,0:T(8,128)(2,1)}), bf16[256,1024]{1,0:T(8,128)(2,1)}) %reduce-scatter.14.cloned.1.call-update) | async-done | bytes 524304 | tf_op jit(solution)/shard_map/reduce_scatter | solution.py:256
  1396.3 19.2 convolution_convert_fusion.1
  1433.9 150.6 %reduce-scatter.28.cloned.1.call-done = bf16[128,6144]{1,0:T(8,128)(2,1)} async-done(((bf16[2048,6144]{1,0:T(8,128)(2,1)}), bf16[128,6144]{1,0:T(8,128)(2,1)}) %reduce-scatter.28.cloned.1.call-update) | async-done | bytes 1572880
  1587.1 101.4 %reduce-scatter.16.cloned.1.call-done = bf16[128,2048]{1,0:T(8,128)(2,1)} async-done(((bf16[2048,2048]{1,0:T(8,128)(2,1)}), bf16[128,2048]{1,0:T(8,128)(2,1)}) %reduce-scatter.16.cloned.1.call-update) | async-done | bytes 524304 | tf_op jit(solution)/shard_map/reduce_scatter | solution.py:49
  1688.5 105.3 %reduce-scatter.22.cloned.1.call-done = bf16[128,2048]{1,0:T(8,128)(2,1)} async-done(((bf16[2048,2048]{1,0:T(8,128)(2,1)}), bf16[128,2048]{1,0:T(8,128)(2,1)}) %reduce-scatter.22.cloned.1.call-update) | async-done | bytes 524304 | tf_op jit(solution)/shard_map/reduce_scatter | solution.py:49
  1793.8 82.8 %reduce-scatter.18.cloned.1.call-done = bf16[128,1024]{1,0:T(8,128)(2,1)} async-done(((bf16[2048,1024]{1,0:T(8,128)(2,1)}), bf16[128,1024]{1,0:T(8,128)(2,1)}) %reduce-scatter.18.cloned.1.call-update) | async-done | bytes 262160 | tf_op jit(solution)/shard_map/reduce_scatter | solution.py:49
  1876.6 83.7 %reduce-scatter.20.cloned.1.call-done = bf16[128,1024]{1,0:T(8,128)(2,1)} async-done(((bf16[2048,1024]{1,0:T(8,128)(2,1)}), bf16[128,1024]{1,0:T(8,128)(2,1)}) %reduce-scatter.20.cloned.1.call-update) | async-done | bytes 262160 | tf_op jit(solution)/shard_map/reduce_scatter | solution.py:49
  1960.3 194.3 %reduce-scatter.24.cloned.1.call-done = bf16[128,6144]{1,0:T(8,128)(2,1)} async-done(((bf16[2048,6144]{1,0:T(8,128)(2,1)}), bf16[128,6144]{1,0:T(8,128)(2,1)}) %reduce-scatter.24.cloned.1.call-update) | async-done | bytes 1572880 | tf_op jit(solution)/shard_map/reduce_scatter | solution.py:49
  2154.6 192.4 %reduce-scatter.26.cloned.1.call-done = bf16[128,6144]{1,0:T(8,128)(2,1)} async-done(((bf16[2048,6144]{1,0:T(8,128)(2,1)}), bf16[128,6144]{1,0:T(8,128)(2,1)}) %reduce-scatter.26.cloned.1.call-update) | async-done | bytes 1572880 | tf_op jit(solution)/shard_map/reduce_scatter | solution.py:49
  2376.1 148.8 %all-reduce.4 = (f32[2048]{0:T(1024)S(1)}, f32[128]{0:T(128)}, f32[128]{0:T(128)}, f32[2048]{0:T(1024)S(1)}) all-reduce(f32[2048]{0:T(1024)S(1)} %get-tuple-element.356, f32[128]{0:T(128)S(1)} %copy-done.52, f32[128]{0:T(128)S(1)} %get-tuple-element.358, f32[2048]{0:T(1024)S(1)} %copy-done.47), channel_id=1, replica_groups=mesh['rep'=8,'shard'=16] {'rep','shard'}, use_global_device_ids=true, to_apply=%region_18.19 | all-reduce | flops 4352 | bytes 34816 | tf_op jit(solution)/shard_map/psum | solution.py:290
  (374 shorter events, 632.7 us)
Async XLA Ops:
  7.2 62.6 %all-gather.14.cloned.1.call-start = ((), (), s32[]{:S(2)}) async-start(), calls=%async_computation.10 | async-start | bytes 4456448 | tf_op jit(solution)/shard_map/all_gather | solution.py:83
  9.1 116.8 %all-gather.18.cloned.1.call-start = ((), (), s32[]{:S(2)}) async-start(), calls=%async_computation.12 | async-start | bytes 4456448 | tf_op jit(solution)/shard_map/all_gather | solution.py:84
  11.0 188.8 %all-gather.12.cloned.1.call-start = ((), (), s32[]{:S(2)}) async-start(), calls=%async_computation.9 | async-start | bytes 8912896 | tf_op jit(solution)/shard_map/all_gather | solution.py:82
  13.2 260.2 %all-gather.16.cloned.1.call-start = ((), (), s32[]{:S(2)}) async-start(), calls=%async_computation.11 | async-start | bytes 8912896 | tf_op jit(solution)/shard_map/all_gather | solution.py:106
  38.9 160.9 %copy-start.30 = (f32[16,1,128]{2,1,0:T(1,128)}, f32[16,1,128]{2,1,0:T(1,128)S(1)}, u32[]{:S(2)}) copy-start(f32[16,1,128]{2,1,0:T(1,128)S(1)} %convert_element_type.240) | copy-start | bytes 24580
  39.8 160.0 %copy-start.39 = (f32[256]{0:T(256)}, f32[256]{0:T(256)S(1)}, u32[]{:S(2)}) copy-start(f32[256]{0:T(256)S(1)} %fusion.64) | copy-start | bytes 3076
  40.3 171.6 %copy-start.19 = (f32[256,64]{1,0:T(8,128)}, f32[256,64]{1,0:T(8,128)S(1)}, u32[]{:S(2)}) copy-start(f32[256,64]{1,0:T(8,128)S(1)} %get-tuple-element.424) | copy-start | bytes 196612
  40.4 171.6 %copy-start.21 = (f32[256,64]{1,0:T(8,128)}, f32[256,64]{1,0:T(8,128)S(1)}, u32[]{:S(2)}) copy-start(f32[256,64]{1,0:T(8,128)S(1)} %get-tuple-element.425) | copy-start | bytes 196612
  76.2 270.9 %all-gather.20.cloned.1.call-start = ((), (), s32[]{:S(2)}) async-start(), calls=%async_computation.13 | async-start | bytes 8912896 | tf_op jit(solution)/shard_map/all_gather | solution.py:107
  130.2 337.3 %all-gather.22.cloned.1.call-start = ((), (), s32[]{:S(2)}) async-start(), calls=%async_computation.14 | async-start | bytes 8912896 | tf_op jit(solution)/shard_map/all_gather | solution.py:85
  131.2 437.4 %all-gather.24.cloned.1.call-start = ((), (), s32[]{:S(2)}) async-start(), calls=%async_computation.15 | async-start | bytes 26738688 | tf_op jit(solution)/shard_map/all_gather | solution.py:161
  134.5 582.3 %all-gather.26.cloned.1.call-start = ((), (), s32[]{:S(2)}) async-start(), calls=%async_computation.16 | async-start | bytes 26738688 | tf_op jit(solution)/shard_map/all_gather | solution.py:162
  137.9 727.1 %all-gather.28.cloned.1.call-start = ((), (), s32[]{:S(2)}) async-start(), calls=%async_computation.17 | async-start | bytes 26738688 | tf_op jit(solution)/shard_map/all_gather | solution.py:172
  141.2 1144.1 %reduce-scatter.12.cloned.1.call-start = ((), (), s32[]{:S(2)}) async-start(), calls=%async_computation.18 | async-start | bytes 8912896 | tf_op jit(solution)/shard_map/reduce_scatter | solution.py:253
  475.4 241.3 %copy-start.9 = (bf16[256,2048]{1,0:T(8,128)(2,1)}, bf16[256,2048]{1,0:T(8,128)(2,1)S(1)}, u32[]{:S(2)}) copy-start(bf16[256,2048]{1,0:T(8,128)(2,1)S(1)} %multiply_convert_fusion.3) | copy-start | bytes 3145732
  1186.7 204.0 %reduce-scatter.14.cloned.1.call-start = ((), (), s32[]{:S(2)}) async-start(), calls=%async_computation.19 | async-start | bytes 8912896 | tf_op jit(solution)/shard_map/reduce_scatter | solution.py:256
  1187.4 397.1 %reduce-scatter.28.cloned.1.call-start = ((), (), s32[]{:S(2)}) async-start(), calls=%async_computation.26 | async-start | bytes 26738688
  1237.3 451.2 %reduce-scatter.16.cloned.1.call-start = ((), (), s32[]{:S(2)}) async-start(), calls=%async_computation.20 | async-start | bytes 8912896 | tf_op jit(solution)/shard_map/reduce_scatter | solution.py:49
  1258.3 535.5 %reduce-scatter.22.cloned.1.call-start = ((), (), s32[]{:S(2)}) async-start(), calls=%async_computation.23 | async-start | bytes 8912896 | tf_op jit(solution)/shard_map/reduce_scatter | solution.py:49
  1266.8 609.8 %reduce-scatter.18.cloned.1.call-start = ((), (), s32[]{:S(2)}) async-start(), calls=%async_computation.21 | async-start | bytes 4456448 | tf_op jit(solution)/shard_map/reduce_scatter | solution.py:49
  1295.7 664.6 %reduce-scatter.20.cloned.1.call-start = ((), (), s32[]{:S(2)}) async-start(), calls=%async_computation.22 | async-start | bytes 4456448 | tf_op jit(solution)/shard_map/reduce_scatter | solution.py:49
  1395.1 759.4 %reduce-scatter.24.cloned.1.call-start = ((), (), s32[]{:S(2)}) async-start(), calls=%async_computation.24 | async-start | bytes 26738688 | tf_op jit(solution)/shard_map/reduce_scatter | solution.py:49
  1415.5 931.5 %reduce-scatter.26.cloned.1.call-start = ((), (), s32[]{:S(2)}) async-start(), calls=%async_computation.25 | async-start | bytes 26738688 | tf_op jit(solution)/shard_map/reduce_scatter | solution.py:49
  1433.8 1095.4 %all-reduce.8.cloned.1.call-start = ((), (), s32[]{:S(2)}) async-start(), calls=%async_computation.27 | async-start | bytes 12582912 | tf_op jit(solution)/shard_map/psum | solution.py:302
  (57 other events, 630.4 us)
Sparse Core Ops, SparseCore 0:
  11.1 58.6 all-gather.13
  72.8 53.0 all-gather.17
  128.9 70.7 all-gather.11
  202.6 70.6 all-gather.15
  276.3 70.6 all-gather.19
  349.3 70.6 all-gather.21
  423.1 145.3 all-gather.23
  571.5 145.1 all-gather.25
  719.8 145.1 all-gather.27
  1186.8 98.4 reduce-scatter.11
  1289.6 101.0 reduce-scatter.13
  1394.9 189.5 reduce-scatter.27
  1588.8 99.6 reduce-scatter.15
  1692.6 101.1 reduce-scatter.21
  1797.6 78.8 reduce-scatter.17
  1881.0 79.2 reduce-scatter.19
  1964.5 190.0 reduce-scatter.23
  2158.8 188.1 reduce-scatter.25
  2350.6 146.2 all-reduce.7
where the time goes:
time: 2560 us; the launch traced here: 2550 us
  waiting for transfers between devices  1630 us (64%)
  matrix products  445 us (17%)
  blocking collectives  194 us (8%)
  other arithmetic  162 us (6%)
  local copies, waits for them, and re-layouts  75.8 us (3%)
    reduce_scatter x6, waiting for transfers between devices, owner_share(): lax.psum_scatter(term.astype(jnp.bfloat16), 'shard', scatter_dimension=0,...  760 us
    unnamed x20, waiting for transfers between devices  152 us
    psum x1, blocking collectives, local(): lax.psum((attn_gain_part, mlp_gain_part, query_gain_part, key_gain_part),...  149 us
    all_gather x1, waiting for transfers between devices, local(): lax.all_gather(down_cast, 'shard', axis=0, tiled=True)  134 us
    all_gather x1, waiting for transfers between devices, local(): up_piece = lax.all_gather(up_cast, 'shard', axis=0, tiled=True)  134 us
    dot_general x16, matrix products, head_scores(): lax.dot_general(query_heads[head_index], head_keys, contract_last, prefer...  96.5 us
    reduce_scatter x1, waiting for transfers between devices, local(): lax.psum_scatter(value_grads.astype(jnp.bfloat16), 'shard', scatter_dimen...  95 us
    all_gather x1, waiting for transfers between devices, local(): gate_piece = lax.all_gather(gate_cast, 'shard', axis=0, tiled=True)  93.1 us
  transfers between devices with their start and end apart: 19, of which 17 were waited for; matrix products, arithmetic and copies ran while one was open for 13% of the time, Pallas kernels for 0%

commit v1 on v0

--- a/solution.py
+++ b/solution.py
@@ -158,8 +158,11 @@
     up_cast = up_weight.astype(jnp.bfloat16)
     down_cast = down_weight.astype(jnp.bfloat16)
     gain_piece = lax.all_gather(mlp_gain.astype(jnp.bfloat16), "shard", axis=0, tiled=True)
-    gate_piece = lax.all_gather(gate_cast, "shard", axis=0, tiled=True)
-    up_piece = lax.all_gather(up_cast, "shard", axis=0, tiled=True)
+    gate_piece, up_piece = jnp.split(
+        lax.all_gather(jnp.concatenate([gate_cast, up_cast], axis=1), "shard", axis=0, tiled=True),
+        [gate_cast.shape[1]],
+        axis=1,
+    )
     columns = second_norm
     piece_in = (columns * gain_piece.astype(jnp.float32)).astype(jnp.bfloat16)
     gate_act = jnp.dot(piece_in, gate_piece, preferred_element_type=jnp.float32)

time: 2560 us -> 2760 us (1.078)
  waiting for transfers between devices: 1630 us -> 1860 us
    all_gather x2 -> x3, waiting for transfers between devices: 227 us -> 470 us  [the longest x1 209 us: local(): lax.all_gather(jnp.concatenate([gate_cast, up_cast], axis=1), 'shard', ax...]
    unnamed x20 -> x21, waiting for transfers between devices: 152 us -> 153 us
  transfers between devices with their start and end apart: 19 -> 20, of which waited for: 17 -> 18; matrix products, arithmetic and copies ran while one was open for 13% -> 14% of each run, Pallas kernels for 0% -> 0%
where the time goes in v1:
time: 2760 us; the launch traced here: 2750 us
  waiting for transfers between devices  1860 us (67%)
  matrix products  419 us (15%)
  blocking collectives  194 us (7%)
  other arithmetic  166 us (6%)
  local copies, waits for them, and re-layouts  74.6 us (3%)
    reduce_scatter x6, waiting for transfers between devices, owner_share(): lax.psum_scatter(term.astype(jnp.bfloat16), 'shard', scatter_dimension=0,...  760 us
    all_gather x1, waiting for transfers between devices, local(): lax.all_gather(jnp.concatenate([gate_cast, up_cast], axis=1), 'shard', ax...  209 us
    unnamed x21, waiting for transfers between devices  153 us
    psum x1, blocking collectives, local(): lax.psum((attn_gain_part, mlp_gain_part, query_gain_part, key_gain_part),...  149 us
    all_gather x1, waiting for transfers between devices, local(): lax.all_gather(up_cast, 'shard', axis=0, tiled=True)  134 us
    all_gather x1, waiting for transfers between devices, local(): lax.all_gather(gate_cast, 'shard', axis=0, tiled=True)  127 us
    all_gather x1, waiting for transfers between devices, local(): lax.all_gather(down_cast, 'shard', axis=0, tiled=True)  121 us
    dot_general x16, matrix products, head_scores(): lax.dot_general(query_heads[head_index], head_keys, contract_last, prefer...  96.3 us
  transfers between devices with their start and end apart: 20, of which 18 were waited for; matrix products, arithmetic and copies ran while one was open for 14% of the time, Pallas kernels for 0%

profile of v1, /device:TPU:1, one launch (start us, length us, event | category | flops | bytes accessed | tf_op | source)
XLA Modules:
  0.0 2753.0 jit_solution(15624104739613901114)
XLA Ops:
  13.2 25.6 all-gather
  40.3 29.4 %all-gather.15.cloned.1.call-done = bf16[2048,1024]{1,0:T(8,128)(2,1)} async-done(((bf16[128,1024]{1,0:T(8,128)(2,1)}), bf16[2048,1024]{1,0:T(8,128)(2,1)}) %all-gather.15.cloned.1.call-update) | async-done | bytes 4194320 | tf_op jit(solution)/shard_map/all_gather | solution.py:83
  76.2 49.7 %all-gather.19.cloned.1.call-done = bf16[2048,1024]{1,0:T(8,128)(2,1)} async-done(((bf16[128,1024]{1,0:T(8,128)(2,1)}), bf16[2048,1024]{1,0:T(8,128)(2,1)}) %all-gather.19.cloned.1.call-update) | async-done | bytes 4194320 | tf_op jit(solution)/shard_map/all_gather | solution.py:84
  145.4 20.0 all-gather.1
  167.7 32.0 %all-gather.13.cloned.1.call-done = bf16[2048,2048]{1,0:T(8,128)(2,1)} async-done(((bf16[128,2048]{1,0:T(8,128)(2,1)}), bf16[2048,2048]{1,0:T(8,128)(2,1)}) %all-gather.13.cloned.1.call-update) | async-done | bytes 8388624 | tf_op jit(solution)/shard_map/all_gather | solution.py:82
  214.9 58.4 %all-gather.17.cloned.1.call-done = bf16[4096,1024]{1,0:T(8,128)(2,1)} async-done(((bf16[256,1024]{1,0:T(8,128)(2,1)}), bf16[4096,1024]{1,0:T(8,128)(2,1)}) %all-gather.17.cloned.1.call-update) | async-done | bytes 8388624 | tf_op jit(solution)/shard_map/all_gather | solution.py:106
  273.4 73.6 %all-gather.21.cloned.1.call-done = bf16[4096,1024]{1,0:T(8,128)(2,1)} async-done(((bf16[256,1024]{1,0:T(8,128)(2,1)}), bf16[4096,1024]{1,0:T(8,128)(2,1)}) %all-gather.21.cloned.1.call-update) | async-done | bytes 8388624 | tf_op jit(solution)/shard_map/all_gather | solution.py:107
  347.0 118.3 %while.33 = (s32[]{:T(128)}, bf16[8,512,128]{2,1,0:T(8,128)(2,1)}, f32[8,512,1]{1,2,0:T(1,128)S(1)}, s32[8]{0:T(128)S(1)}, bf16[8,512,128]{2,1,0:T(8,128)(2,1)},...) while((s32[]{:T(128)}, bf16[8,512,128]{2,1,0:T(8,128)(2,1)}, ...), condition=%wide.region_6.7_spmd.clone.clone, body=%wide.region_3.6_spmd.clone.sunk.clone | while | flops 1098907136 | bytes 39211212 | solution.py:145
  475.4 208.8 %all-gather.25.cloned.1.call-done = bf16[2048,12288]{1,0:T(8,128)(2,1)} async-done(((bf16[128,12288]{1,0:T(8,128)(2,1)}), bf16[2048,12288]{1,0:T(8,128)(2,1)}) %all-gather.25.cloned.1.call-update) | async-done | bytes 50331664 | tf_op jit(solution)/shard_map/all_gather | solution.py:162
  711.4 120.8 %all-gather.27.cloned.1.call-done = bf16[2048,6144]{1,0:T(8,128)(2,1)} async-done(((bf16[128,6144]{1,0:T(8,128)(2,1)}), bf16[2048,6144]{1,0:T(8,128)(2,1)}) %all-gather.27.cloned.1.call-update) | async-done | bytes 25165840 | tf_op jit(solution)/shard_map/all_gather | solution.py:175
  832.2 20.4 multiply_convert_fusion.1
  852.7 127.2 %all-gather.29.cloned.1.call-done = bf16[2048,6144]{1,0:T(8,128)(2,1)} async-done(((bf16[128,6144]{1,0:T(8,128)(2,1)}), bf16[2048,6144]{1,0:T(8,128)(2,1)}) %all-gather.29.cloned.1.call-update) | async-done | bytes 25165840 | tf_op jit(solution)/shard_map/all_gather | solution.py:192
  993.6 133.8 %all-gather.31.cloned.1.call-done = bf16[2048,6144]{1,0:T(8,128)(2,1)} async-done(((bf16[128,6144]{1,0:T(8,128)(2,1)}), bf16[2048,6144]{1,0:T(8,128)(2,1)}) %all-gather.31.cloned.1.call-update) | async-done | bytes 25165840 | tf_op jit(solution)/shard_map/all_gather | solution.py:197
  1164.7 225.9 %while.34 = (s32[]{:T(128)}, f32[8,512,128]{2,1,0:T(8,128)}, bf16[4096,1024]{1,0:T(8,128)(2,1)}, bf16[4096,1024]{1,0:T(8,128)(2,1)}, bf16[8,512,128]{2,1,0:T(8,1...) while((s32[]{:T(128)}, f32[8,512,128]{2,1,0:T(8,128)}, ...), condition=%wide.region_11.12_spmd.clone.clone, body=%wide.region_9.11_spmd.clone.sunk.clone | while | flops 2703818240 | bytes 139208960 | solution.py:254
  1408.4 31.6 %copy.74 = bf16[2048,6144]{1,0:T(8,128)(2,1)} copy(bf16[2048,6144]{0,1:T(8,128)(2,1)} %convert_bitcast_fusion) | data formatting | bytes 50331648
  1499.8 94.8 %reduce-scatter.14.cloned.1.call-done = bf16[256,1024]{1,0:T(8,128)(2,1)} async-done(((bf16[4096,1024]{1,0:T(8,128)(2,1)}), bf16[256,1024]{1,0:T(8,128)(2,1)}) %reduce-scatter.14.cloned.1.call-update) | async-done | bytes 524304 | tf_op jit(solution)/shard_map/reduce_scatter | solution.py:259
  1637.7 150.7 %reduce-scatter.28.cloned.1.call-done = bf16[128,6144]{1,0:T(8,128)(2,1)} async-done(((bf16[2048,6144]{1,0:T(8,128)(2,1)}), bf16[128,6144]{1,0:T(8,128)(2,1)}) %reduce-scatter.28.cloned.1.call-update) | async-done | bytes 1572880
  1791.0 101.3 %reduce-scatter.16.cloned.1.call-done = bf16[128,2048]{1,0:T(8,128)(2,1)} async-done(((bf16[2048,2048]{1,0:T(8,128)(2,1)}), bf16[128,2048]{1,0:T(8,128)(2,1)}) %reduce-scatter.16.cloned.1.call-update) | async-done | bytes 524304 | tf_op jit(solution)/shard_map/reduce_scatter | solution.py:49
  1892.3 105.3 %reduce-scatter.22.cloned.1.call-done = bf16[128,2048]{1,0:T(8,128)(2,1)} async-done(((bf16[2048,2048]{1,0:T(8,128)(2,1)}), bf16[128,2048]{1,0:T(8,128)(2,1)}) %reduce-scatter.22.cloned.1.call-update) | async-done | bytes 524304 | tf_op jit(solution)/shard_map/reduce_scatter | solution.py:49
  1997.6 82.8 %reduce-scatter.18.cloned.1.call-done = bf16[128,1024]{1,0:T(8,128)(2,1)} async-done(((bf16[2048,1024]{1,0:T(8,128)(2,1)}), bf16[128,1024]{1,0:T(8,128)(2,1)}) %reduce-scatter.18.cloned.1.call-update) | async-done | bytes 262160 | tf_op jit(solution)/shard_map/reduce_scatter | solution.py:49
  2080.5 83.7 %reduce-scatter.20.cloned.1.call-done = bf16[128,1024]{1,0:T(8,128)(2,1)} async-done(((bf16[2048,1024]{1,0:T(8,128)(2,1)}), bf16[128,1024]{1,0:T(8,128)(2,1)}) %reduce-scatter.20.cloned.1.call-update) | async-done | bytes 262160 | tf_op jit(solution)/shard_map/reduce_scatter | solution.py:49
  2164.2 194.1 %reduce-scatter.24.cloned.1.call-done = bf16[128,6144]{1,0:T(8,128)(2,1)} async-done(((bf16[2048,6144]{1,0:T(8,128)(2,1)}), bf16[128,6144]{1,0:T(8,128)(2,1)}) %reduce-scatter.24.cloned.1.call-update) | async-done | bytes 1572880 | tf_op jit(solution)/shard_map/reduce_scatter | solution.py:49
  2358.3 192.4 %reduce-scatter.26.cloned.1.call-done = bf16[128,6144]{1,0:T(8,128)(2,1)} async-done(((bf16[2048,6144]{1,0:T(8,128)(2,1)}), bf16[128,6144]{1,0:T(8,128)(2,1)}) %reduce-scatter.26.cloned.1.call-update) | async-done | bytes 1572880 | tf_op jit(solution)/shard_map/reduce_scatter | solution.py:49
  2579.8 148.6 %all-reduce.4 = (f32[2048]{0:T(1024)S(1)}, f32[128]{0:T(128)}, f32[128]{0:T(128)}, f32[2048]{0:T(1024)S(1)}) all-reduce(f32[2048]{0:T(1024)S(1)} %get-tuple-element.356, f32[128]{0:T(128)S(1)} %copy-done.53, f32[128]{0:T(128)S(1)} %get-tuple-element.358, f32[2048]{0:T(1024)S(1)} %copy-done.48), channel_id=1, replica_groups=mesh['rep'=8,'shard'=16] {'rep','shard'}, use_global_device_ids=true, to_apply=%region_18.19 | all-reduce | flops 4352 | bytes 34816 | tf_op jit(solution)/shard_map/psum | solution.py:293
  (394 shorter events, 630.7 us)
Async XLA Ops:
  7.2 62.6 %all-gather.15.cloned.1.call-start = ((), (), s32[]{:S(2)}) async-start(), calls=%async_computation.10 | async-start | bytes 4456448 | tf_op jit(solution)/shard_map/all_gather | solution.py:83
  9.1 116.8 %all-gather.19.cloned.1.call-start = ((), (), s32[]{:S(2)}) async-start(), calls=%async_computation.12 | async-start | bytes 4456448 | tf_op jit(solution)/shard_map/all_gather | solution.py:84
  11.0 188.7 %all-gather.13.cloned.1.call-start = ((), (), s32[]{:S(2)}) async-start(), calls=%async_computation.9 | async-start | bytes 8912896 | tf_op jit(solution)/shard_map/all_gather | solution.py:82
  13.2 260.2 %all-gather.17.cloned.1.call-start = ((), (), s32[]{:S(2)}) async-start(), calls=%async_computation.11 | async-start | bytes 8912896 | tf_op jit(solution)/shard_map/all_gather | solution.py:106
  38.9 160.9 %copy-start.34 = (f32[16,1,128]{2,1,0:T(1,128)}, f32[16,1,128]{2,1,0:T(1,128)S(1)}, u32[]{:S(2)}) copy-start(f32[16,1,128]{2,1,0:T(1,128)S(1)} %convert_element_type.240) | copy-start | bytes 24580
  40.3 171.6 %copy-start.21 = (f32[256,64]{1,0:T(8,128)}, f32[256,64]{1,0:T(8,128)S(1)}, u32[]{:S(2)}) copy-start(f32[256,64]{1,0:T(8,128)S(1)} %get-tuple-element.424) | copy-start | bytes 196612
  40.3 171.6 %copy-start.23 = (f32[256,64]{1,0:T(8,128)}, f32[256,64]{1,0:T(8,128)S(1)}, u32[]{:S(2)}) copy-start(f32[256,64]{1,0:T(8,128)S(1)} %get-tuple-element.425) | copy-start | bytes 196612
  76.2 270.8 %all-gather.21.cloned.1.call-start = ((), (), s32[]{:S(2)}) async-start(), calls=%async_computation.13 | async-start | bytes 8912896 | tf_op jit(solution)/shard_map/all_gather | solution.py:107
  130.2 337.3 %all-gather.23.cloned.1.call-start = ((), (), s32[]{:S(2)}) async-start(), calls=%async_computation.14 | async-start | bytes 8912896 | tf_op jit(solution)/shard_map/all_gather | solution.py:85
  131.2 553.1 %all-gather.25.cloned.1.call-start = ((), (), s32[]{:S(2)}) async-start(), calls=%async_computation.15 | async-start | bytes 53477376 | tf_op jit(solution)/shard_map/all_gather | solution.py:162
  140.6 691.6 %all-gather.27.cloned.1.call-start = ((), (), s32[]{:S(2)}) async-start(), calls=%async_computation.16 | async-start | bytes 26738688 | tf_op jit(solution)/shard_map/all_gather | solution.py:175
  143.9 836.0 %all-gather.29.cloned.1.call-start = ((), (), s32[]{:S(2)}) async-start(), calls=%async_computation.17 | async-start | bytes 26738688 | tf_op jit(solution)/shard_map/all_gather | solution.py:192
  144.6 982.7 %all-gather.31.cloned.1.call-start = ((), (), s32[]{:S(2)}) async-start(), calls=%async_computation.18 | async-start | bytes 26738688 | tf_op jit(solution)/shard_map/all_gather | solution.py:197
  145.2 1344.0 %reduce-scatter.12.cloned.1.call-start = ((), (), s32[]{:S(2)}) async-start(), calls=%async_computation.19 | async-start | bytes 8912896 | tf_op jit(solution)/shard_map/reduce_scatter | solution.py:256
  475.4 222.6 %copy-start.11 = (bf16[256,2048]{1,0:T(8,128)(2,1)}, bf16[256,2048]{1,0:T(8,128)(2,1)S(1)}, u32[]{:S(2)}) copy-start(bf16[256,2048]{1,0:T(8,128)(2,1)S(1)} %multiply_convert_fusion.3) | copy-start | bytes 3145732
  1390.6 203.9 %reduce-scatter.14.cloned.1.call-start = ((), (), s32[]{:S(2)}) async-start(), calls=%async_computation.20 | async-start | bytes 8912896 | tf_op jit(solution)/shard_map/reduce_scatter | solution.py:259
  1391.2 397.3 %reduce-scatter.28.cloned.1.call-start = ((), (), s32[]{:S(2)}) async-start(), calls=%async_computation.27 | async-start | bytes 26738688
  1440.1 452.2 %reduce-scatter.16.cloned.1.call-start = ((), (), s32[]{:S(2)}) async-start(), calls=%async_computation.21 | async-start | bytes 8912896 | tf_op jit(solution)/shard_map/reduce_scatter | solution.py:49
  1460.8 536.8 %reduce-scatter.22.cloned.1.call-start = ((), (), s32[]{:S(2)}) async-start(), calls=%async_computation.24 | async-start | bytes 8912896 | tf_op jit(solution)/shard_map/reduce_scatter | solution.py:49
  1469.3 611.2 %reduce-scatter.18.cloned.1.call-start = ((), (), s32[]{:S(2)}) async-start(), calls=%async_computation.22 | async-start | bytes 4456448 | tf_op jit(solution)/shard_map/reduce_scatter | solution.py:49
  1499.7 664.5 %reduce-scatter.20.cloned.1.call-start = ((), (), s32[]{:S(2)}) async-start(), calls=%async_computation.23 | async-start | bytes 4456448 | tf_op jit(solution)/shard_map/reduce_scatter | solution.py:49
  1599.0 759.3 %reduce-scatter.24.cloned.1.call-start = ((), (), s32[]{:S(2)}) async-start(), calls=%async_computation.25 | async-start | bytes 26738688 | tf_op jit(solution)/shard_map/reduce_scatter | solution.py:49
  1619.2 931.5 %reduce-scatter.26.cloned.1.call-start = ((), (), s32[]{:S(2)}) async-start(), calls=%async_computation.26 | async-start | bytes 26738688 | tf_op jit(solution)/shard_map/reduce_scatter | solution.py:49
  1637.7 1095.1 %all-reduce.8.cloned.1.call-start = ((), (), s32[]{:S(2)}) async-start(), calls=%async_computation.28 | async-start | bytes 12582912 | tf_op jit(solution)/shard_map/psum | solution.py:305
  (66 other events, 847.3 us)
Sparse Core Ops, SparseCore 0:
  11.1 58.6 all-gather.14
  72.8 53.0 all-gather.18
  128.9 70.7 all-gather.12
  202.6 70.6 all-gather.16
  276.3 70.6 all-gather.20
  349.9 70.6 all-gather.22
  423.7 260.5 all-gather.24
  687.3 144.8 all-gather.26
  834.7 145.1 all-gather.28
  982.2 145.1 all-gather.30
  1390.7 98.4 reduce-scatter.11
  1493.4 101.1 reduce-scatter.13
  1598.9 189.5 reduce-scatter.27
  1792.6 99.6 reduce-scatter.15
  1896.4 101.1 reduce-scatter.21
  2001.5 78.9 reduce-scatter.17
  2084.8 79.3 reduce-scatter.19
  2168.4 189.8 reduce-scatter.23
  2362.6 188.0 reduce-scatter.25
  2554.2 146.3 all-reduce.7
